TPU v7x, 128 devices: a whole 4x4x4 slice. The times are simulated.
128 devices in a mesh: space: 32 (over z, x, core), head: 4 (over y).
Axes of the slice: x: 4, y: 4, z: 4, core: 2. Of those that a mesh axis runs over, the one named last changes fastest.
Arguments:
- tokens: bfloat16 [32768, 1024], P('space'), may hold values from -70 to 70
- w_qkv: bfloat16 [1024, 3, 1024], P(None, None, 'head'), may hold values from -7 to 7
- w_out: bfloat16 [1024, 1024], P('head'), may hold values from -0.5 to 0.5
- neighbours: int32 [256, 9], P('space'), may hold values from 0 to 71, as said below
- requests: int32 [32, 32, 2], P('space'), may hold values from -1 to 7, as said below
- cotangent: bfloat16 [32768, 1024], P('space', 'head'), may hold values from -6 to 6
Outputs:
- layer_out: bfloat16 [32768, 1024], P('space', 'head')
- grad_tokens: bfloat16 [32768, 1024], P('space', 'head')
- grad_w_qkv: float32 [1024, 3, 1024], P('space', None, 'head')
- grad_w_out: float32 [1024, 1024], P('head', 'space')
Inputs may be any that keep to these rules, and one draw needn't show every extreme that they name: `neighbours`: row t starts with t % 8 itself, then 3 other tiles of the same device, then 5 slot entries 8 + p * 2 + c; every slot entry names a filled request of that device, every filled request is named by some tile of that device, and no row names a tile twice. requests[d, p, c] is a tile of device p by its index within p, or -1 for an empty slot; filled slots come first and are distinct, requests[d, d] is empty, and in every draw some device fills all 2 slots towards some other device.
All inputs are finite; a program needn't handle non-finite values.
Results may differ from a plain program's by a relative error of at most 0.02.
The roundings to bfloat16 on the way count: a program that leaves them out, or rounds other values in their place, can miss the bound.
Values may be sent and summed in bfloat16 or wider, within the bound.
A program may use at most 192 MiB of HBM per device.

v0:
```python
import jax
import jax.numpy as jnp
from jax import lax
from jax.sharding import PartitionSpec as P

HEAD_DIM = 64
BLOCK_TILES = 4
NEIGHBOURS = 9
EPSILON = 1e-05


def norm_parts(tokens):
    values = tokens.astype(jnp.float32)
    centred = values - jnp.mean(values, axis=1, keepdims=True)
    inverse = lax.rsqrt(jnp.mean(centred * centred, axis=1, keepdims=True) + EPSILON)
    return (centred * inverse, inverse)


def gather_keys(extended, block_entries, head_count):
    entry_count = block_entries.shape[0]
    tile_rows = extended.shape[2]
    picked = jnp.take(extended, block_entries.reshape(-1), axis=1)
    return picked.reshape(2, entry_count, NEIGHBOURS * tile_rows, head_count, HEAD_DIM)


def probabilities(queries, key_part, score_scale):
    scores = (
        jnp.einsum("bihe,bjhe->bhij", queries, key_part, preferred_element_type=jnp.float32)
        * score_scale
    )
    row_top = jnp.max(scores, axis=3, keepdims=True)
    weights = jnp.exp(scores - row_top)
    return weights / jnp.sum(weights, axis=3, keepdims=True)


def select_pairs(local_pairs, incoming):
    peer_count, slot_count = incoming.shape
    flat_wanted = incoming.reshape(-1)
    usable = (flat_wanted >= 0)[None, :, None, None]
    picked = jnp.take(local_pairs, jnp.maximum(flat_wanted, 0), axis=1)
    picked = jnp.where(usable, picked, jnp.zeros_like(picked))
    return picked.reshape(2, peer_count, slot_count, local_pairs.shape[2], local_pairs.shape[3])


def on_device(tokens, w_qkv, w_out, neighbours, requests, cotangent):
    row_count, model_width = tokens.shape
    tile_count = neighbours.shape[0]
    tile_rows = row_count // tile_count
    head_width = w_qkv.shape[2]
    head_count = head_width // HEAD_DIM
    peer_count = lax.axis_size("space")
    slot_count = requests.shape[2]
    col_share = cotangent.shape[1]
    column = lax.axis_index("head") * col_share
    score_scale = HEAD_DIM ** (-0.5)
    block_count = tile_count // BLOCK_TILES
    extent = tile_count + peer_count * slot_count
    standard, inverse = norm_parts(tokens)
    normed = standard.astype(jnp.bfloat16)
    flat_weight = w_qkv.reshape(model_width, 3 * head_width)
    projected = jnp.dot(normed, flat_weight, preferred_element_type=jnp.float32).astype(
        jnp.bfloat16
    )
    queries = projected[:, :head_width].reshape(
        block_count, BLOCK_TILES, tile_rows, head_count, HEAD_DIM
    )
    local_pairs = jnp.transpose(
        projected[:, head_width:].reshape(row_count, 2, head_width), (1, 0, 2)
    )
    local_pairs = local_pairs.reshape(2, tile_count, tile_rows, head_width)
    entries = neighbours.reshape(block_count, BLOCK_TILES, NEIGHBOURS)
    incoming = lax.all_to_all(
        requests.reshape(peer_count, slot_count), "space", split_axis=0, concat_axis=0, tiled=True
    )
    outgoing = select_pairs(local_pairs, incoming)
    fetched, incoming = (
        lax.all_to_all(outgoing, "space", split_axis=1, concat_axis=1, tiled=True),
        incoming,
    )
    extended = jnp.concatenate(
        [local_pairs, fetched.reshape(2, peer_count * slot_count, tile_rows, head_width)], 1
    )

    def forward_block(inputs):
        block_queries, block_entries = inputs
        keyset = gather_keys(extended, block_entries, head_count)
        likely = probabilities(block_queries, keyset[0], score_scale)
        rounded = likely.astype(jnp.bfloat16)
        mixed = jnp.einsum(
            "bhij,bjhe->bihe", rounded, keyset[1], preferred_element_type=jnp.float32
        )
        return mixed.astype(jnp.bfloat16)

    attended = lax.map(forward_block, (queries, entries)).reshape(row_count, head_width)
    partial_out = jnp.dot(attended, w_out, preferred_element_type=jnp.float32)
    summed = lax.psum_scatter(
        partial_out.astype(jnp.bfloat16), "head", scatter_dimension=1, tiled=True
    ).astype(jnp.float32)
    own_tokens = lax.dynamic_slice_in_dim(tokens, column, col_share, 1).astype(jnp.float32)
    layer_out = (own_tokens + summed).astype(jnp.bfloat16)
    cotangent_full = lax.all_gather(cotangent, "head", axis=1, tiled=True)
    grad_attended = jnp.einsum(
        "td,fd->tf", cotangent_full, w_out, preferred_element_type=jnp.float32
    ).astype(jnp.bfloat16)
    grad_blocks = grad_attended.reshape(block_count, BLOCK_TILES, tile_rows, head_count, HEAD_DIM)
    resent = lax.all_to_all(
        select_pairs(local_pairs, incoming), "space", split_axis=1, concat_axis=1, tiled=True
    )
    backward_keys = jnp.concatenate(
        [local_pairs, resent.reshape(2, peer_count * slot_count, tile_rows, head_width)], 1
    )

    def backward_block(totals, triple):
        block_queries, block_entries, block_grads = triple
        keyset = gather_keys(backward_keys, block_entries, head_count)
        key_part = keyset[0]
        value_part = keyset[1]
        likely = probabilities(block_queries, key_part, score_scale)
        rounded = likely.astype(jnp.bfloat16)
        grad_prob = jnp.einsum(
            "bihe,bjhe->bhij", block_grads, value_part, preferred_element_type=jnp.float32
        )
        row_delta = jnp.sum(likely * grad_prob, axis=3, keepdims=True)
        grad_score = (likely * (grad_prob - row_delta) * score_scale).astype(jnp.bfloat16)
        grad_query = jnp.einsum(
            "bhij,bjhe->bihe", grad_score, key_part, preferred_element_type=jnp.float32
        )
        grad_key = jnp.einsum(
            "bhij,bihe->bjhe", grad_score, block_queries, preferred_element_type=jnp.float32
        )
        grad_value = jnp.einsum(
            "bhij,bihe->bjhe", rounded, block_grads, preferred_element_type=jnp.float32
        )
        entry_count = block_entries.shape[0] * NEIGHBOURS
        flat_entries = block_entries.reshape(-1)
        both_grads = jnp.stack(
            [grad_key.reshape(entry_count, -1), grad_value.reshape(entry_count, -1)], 0
        )
        return (totals.at[:, flat_entries].add(both_grads), grad_query)

    empty_total = jnp.zeros((2, extent, tile_rows * head_width), jnp.float32)
    pair_totals, query_grads = lax.scan(
        backward_block, empty_total, (queries, entries, grad_blocks)
    )
    near_part = pair_totals[:, :tile_count]
    far_part = (
        pair_totals[:, tile_count:]
        .astype(jnp.bfloat16)
        .reshape(2, peer_count, slot_count, tile_rows, head_width)
    )
    returned = lax.all_to_all(far_part, "space", split_axis=1, concat_axis=1, tiled=True)
    placer = (jnp.arange(tile_count, dtype=jnp.int32)[:, None] == incoming.reshape(1, -1)).astype(
        jnp.float32
    )
    landed = jnp.einsum(
        "tp,gpx->gtx",
        placer,
        returned.reshape(2, peer_count * slot_count, -1).astype(jnp.float32),
        precision=lax.Precision.HIGHEST,
    )
    pair_grads = (near_part + landed).reshape(2, row_count, head_width)
    grad_qkv = jnp.concatenate(
        [query_grads.reshape(1, row_count, head_width), pair_grads], 0
    ).astype(jnp.bfloat16)
    normed_rows = normed.T
    cotangent_rows = cotangent_full.T
    input_part = jnp.einsum(
        "ct,gtf->cgf", normed_rows, grad_qkv, preferred_element_type=jnp.float32
    )
    output_part = jnp.dot(cotangent_rows, attended, preferred_element_type=jnp.float32)
    stacked_grads = lax.psum_scatter(
        jnp.concatenate(
            [
                input_part.reshape(
                    model_width // peer_count * lax.axis_size("space"), 3 * head_width
                ),
                output_part,
            ],
            1,
        ).astype(jnp.bfloat16),
        "space",
        scatter_dimension=0,
        tiled=True,
    ).astype(jnp.float32)
    grad_w_qkv = stacked_grads[:, : 3 * head_width].reshape(-1, 3, head_width)
    grad_w_out = stacked_grads[:, 3 * head_width :].T
    grad_normed = jnp.einsum("gtf,dgf->td", grad_qkv, w_qkv, preferred_element_type=jnp.float32)
    own_standard = lax.dynamic_slice_in_dim(standard, column, col_share, 1)
    own_part = lax.psum_scatter(
        grad_normed.astype(jnp.bfloat16), "head", scatter_dimension=1, tiled=True
    ).astype(jnp.float32)
    row_sums = lax.psum(
        (jnp.sum(own_part, axis=1), jnp.sum(own_part * own_standard, axis=1)), "head"
    )
    first_mean = (row_sums[0] / model_width)[:, None]
    second_mean = (row_sums[1] / model_width)[:, None]
    cotangent_wide = cotangent.astype(jnp.float32)
    grad_tokens = (
        cotangent_wide + inverse * (own_part - first_mean - own_standard * second_mean)
    ).astype(jnp.bfloat16)
    return (layer_out, grad_tokens, grad_w_qkv, grad_w_out)


def solution(mesh):
    placed = (
        P("space", None),
        P(None, None, "head"),
        P("head", None),
        P("space", None),
        P("space", None, None),
        P("space", "head"),
    )
    return jax.shard_map(
        on_device,
        mesh=mesh,
        in_specs=placed,
        out_specs=(
            P("space", "head"),
            P("space", "head"),
            P("space", None, "head"),
            P("head", "space"),
        ),
        check_vma=False,
    )
```

profile of v0, /device:TPU:0, one launch (start us, length us, event | category | flops | bytes accessed | tf_op | source)
XLA Modules:
  0.0 916.5 jit_solution(7193930980082506994)
XLA Ops:
  8.7 8.2 all-to-all-start
  35.6 7.6 bitcast_select_fusion
  43.2 7.7 copy.127
  51.0 7.7 all-to-all-start.1
  60.7 36.5 %all-gather.2.cloned.1.call-done = bf16[1024,1024]{1,0:T(8,128)(2,1)} async-done(((bf16[1024,256]{1,0:T(8,128)(2,1)}), bf16[1024,1024]{1,0:T(8,128)(2,1)}) %all-gather.2.cloned.1.call-update) | async-done | bytes 2097168 | tf_op jit(solution)/shard_map/all_gather | solution.py:101
  100.5 64.0 %all-to-all-done.1 = bf16[2,32,2,128,256]{4,3,2,0,1:T(8,128)(2,1)} async-done(((bf16[2,32,2,128,256]{4,3,2,0,1:T(8,128)(2,1)}), bf16[2,32,2,128,256]{4,3,2,0,1:T(8,128)(2,1)}, u32[]{:S(2)}, u32[]{:S(2)}) %all-to-all-start.1) | async-done | bytes 8388640 | tf_op jit(solution)/shard_map/all_to_all | solution.py:77
  164.5 7.8 copy.128
  172.3 7.8 pad_maximum_fusion
  186.9 408.7 %while.23 = (s32[]{:T(128)}, f32[2,72,32768]{2,0,1:T(2,128)}, bf16[2,4,128,4,64]{2,4,3,1,0:T(8,128)(2,1)}, s32[2,4,9]{2,1,0:T(4,128)S(1)}, bf16[2,4,128,4,64]{2,...) while((s32[]{:T(128)}, f32[2,72,32768]{2,0,1:T(2,128)}, ...), condition=%wide.region_12.15_spmd, body=%wide.region_7.14_spmd.sunk | while | flops 1868574720 | bytes 270851232 | solution.py:142
  187.2 8.2 gather_fusion.1
  200.1 8.0 reshape.262
  208.1 7.5 copy.197
  219.7 7.8 fusion.195
  234.8 23.7 %fusion.197 = bf16[2,4,128,4,64]{2,4,3,1,0:T(8,128)(2,1)} fusion(bf16[2,4,128,4,64]{2,4,3,1,0:T(8,128)(2,1)} %get-tuple-element.308, s32[]{:T(128)S(6)} %copy.213, bf16[4,1152,4,64]{1,3,2,0:T(8,128)(2,1)S(1)} %copy-done.1, f32[4,4,128,1152]{3,2,1,0:T(8,128)} %fusion.195, f32[4,4,128,1152]{3,2,1,0:T(8,128)} %get-tuple-element.279, ...), kind=kOutput, calls=%fused_computation.52.clone.1 | convolution fusion | flops 318508160 | bytes 40648708 | tf_op jit(solution)/shard_map/while/body/eval_jaxpr/bhij,bjhe->bihe/dot_general | solution.py:125
  258.5 25.1 %fusion.196 = f32[4,1152,4,64]{1,3,2,0:T(8,128)} fusion(f32[4,4,128,1152]{3,2,1,0:T(8,128)} %fusion.195, bf16[2,4,128,4,64]{2,4,3,1,0:T(8,128)(2,1)} %get-tuple-element.318, s32[]{:T(128)S(6)} %copy.213, f32[4,4,128,1152]{3,2,1,0:T(8,128)} %get-tuple-element.279, f32[4,4,128]{2,1,0:T(4,128)S(1)} %get-tuple-element.277), kind=kOutput, calls=%fused_computation.50.clone.1 | convolution fusion | flops 318508160 | bytes 42745860 | tf_op jit(solution)/shard_map/while/body/eval_jaxpr/bhij,bihe->bjhe/dot_general | solution.py:128
  289.9 9.5 %copy.198 = f32[4,1152,4,64]{3,2,1,0:T(4,128)} copy(f32[4,1152,4,64]{1,3,2,0:T(8,128)} %fusion.194) | data formatting | bytes 9437184 | tf_op jit(solution)/shard_map/while/body/eval_jaxpr/bhij,bihe->bjhe/transpose | solution.py:131
  299.4 10.3 %reshape.263 = f32[1,36,32768]{2,1,0:T(8,128)} reshape(f32[4,1152,4,64]{3,2,1,0:T(4,128)} %copy.198) | data formatting | bytes 9437184 | tf_op jit(solution)/shard_map/while/body/eval_jaxpr/stack;while/body/eval_jaxpr/reshape | solution.py:136
  309.7 9.5 %copy.199 = f32[4,1152,4,64]{3,2,1,0:T(4,128)} copy(f32[4,1152,4,64]{1,3,2,0:T(8,128)} %fusion.196) | data formatting | bytes 9437184 | tf_op jit(solution)/shard_map/while/body/eval_jaxpr/bhij,bihe->bjhe/transpose | solution.py:128
  319.3 10.3 %reshape.265 = f32[1,36,32768]{2,1,0:T(8,128)} reshape(f32[4,1152,4,64]{3,2,1,0:T(4,128)} %copy.199) | data formatting | bytes 9437184 | tf_op jit(solution)/shard_map/while/body/eval_jaxpr/stack;while/body/eval_jaxpr/reshape | solution.py:136
  334.4 7.9 copy.200
  342.3 48.8 %scatter_fusion = f32[2,72,32768]{2,0,1:T(2,128)} fusion(f32[2,72,32768]{2,0,1:T(2,128)} %get-tuple-element.307, s32[36]{0:T(128)S(1)} %fusion.191, f32[36,2,32768]{2,1,0:T(2,128)} %copy.200), kind=kCustom, calls=%fused_computation.3.clone.1 | custom fusion | flops 2359296 | bytes 28311696 | tf_op jit(solution)/shard_map/while/body/eval_jaxpr/scatter-add | solution.py:139
  391.3 8.2 gather_fusion.1
  404.2 8.0 reshape.262
  423.8 7.8 fusion.195
  438.8 23.7 %fusion.197 = bf16[2,4,128,4,64]{2,4,3,1,0:T(8,128)(2,1)} fusion(bf16[2,4,128,4,64]{2,4,3,1,0:T(8,128)(2,1)} %get-tuple-element.308, s32[]{:T(128)S(6)} %copy.213, bf16[4,1152,4,64]{1,3,2,0:T(8,128)(2,1)S(1)} %copy-done.1, f32[4,4,128,1152]{3,2,1,0:T(8,128)} %fusion.195, f32[4,4,128,1152]{3,2,1,0:T(8,128)} %get-tuple-element.279, ...), kind=kOutput, calls=%fused_computation.52.clone.1 | convolution fusion | flops 318508160 | bytes 40648708 | tf_op jit(solution)/shard_map/while/body/eval_jaxpr/bhij,bjhe->bihe/dot_general | solution.py:125
  462.6 25.1 %fusion.196 = f32[4,1152,4,64]{1,3,2,0:T(8,128)} fusion(f32[4,4,128,1152]{3,2,1,0:T(8,128)} %fusion.195, bf16[2,4,128,4,64]{2,4,3,1,0:T(8,128)(2,1)} %get-tuple-element.318, s32[]{:T(128)S(6)} %copy.213, f32[4,4,128,1152]{3,2,1,0:T(8,128)} %get-tuple-element.279, f32[4,4,128]{2,1,0:T(4,128)S(1)} %get-tuple-element.277), kind=kOutput, calls=%fused_computation.50.clone.1 | convolution fusion | flops 318508160 | bytes 42745860 | tf_op jit(solution)/shard_map/while/body/eval_jaxpr/bhij,bihe->bjhe/dot_general | solution.py:128
  493.9 9.5 %copy.198 = f32[4,1152,4,64]{3,2,1,0:T(4,128)} copy(f32[4,1152,4,64]{1,3,2,0:T(8,128)} %fusion.194) | data formatting | bytes 9437184 | tf_op jit(solution)/shard_map/while/body/eval_jaxpr/bhij,bihe->bjhe/transpose | solution.py:131
  503.5 10.3 %reshape.263 = f32[1,36,32768]{2,1,0:T(8,128)} reshape(f32[4,1152,4,64]{3,2,1,0:T(4,128)} %copy.198) | data formatting | bytes 9437184 | tf_op jit(solution)/shard_map/while/body/eval_jaxpr/stack;while/body/eval_jaxpr/reshape | solution.py:136
  513.8 9.5 %copy.199 = f32[4,1152,4,64]{3,2,1,0:T(4,128)} copy(f32[4,1152,4,64]{1,3,2,0:T(8,128)} %fusion.196) | data formatting | bytes 9437184 | tf_op jit(solution)/shard_map/while/body/eval_jaxpr/bhij,bihe->bjhe/transpose | solution.py:128
  523.3 10.3 %reshape.265 = f32[1,36,32768]{2,1,0:T(8,128)} reshape(f32[4,1152,4,64]{3,2,1,0:T(4,128)} %copy.199) | data formatting | bytes 9437184 | tf_op jit(solution)/shard_map/while/body/eval_jaxpr/stack;while/body/eval_jaxpr/reshape | solution.py:136
  538.4 7.9 copy.200
  546.3 48.8 %scatter_fusion = f32[2,72,32768]{2,0,1:T(2,128)} fusion(f32[2,72,32768]{2,0,1:T(2,128)} %get-tuple-element.307, s32[36]{0:T(128)S(1)} %fusion.191, f32[36,2,32768]{2,1,0:T(2,128)} %copy.200), kind=kCustom, calls=%fused_computation.3.clone.1 | custom fusion | flops 2359296 | bytes 28311696 | tf_op jit(solution)/shard_map/while/body/eval_jaxpr/scatter-add | solution.py:139
  595.5 9.4 %slice.60 = bf16[2,64,32768]{2,0,1:T(2,128)(2,1)} slice(f32[2,72,32768]{2,0,1:T(2,128)} %get-tuple-element.73), slice={[0:2], [8:72], [0:32768]} | slice | bytes 16777216 | tf_op jit(solution)/shard_map/slice | solution.py:147
  604.9 14.0 %reshape.225 = bf16[2,32,2,128,256]{4,3,0,2,1:T(8,128)(2,1)} reshape(bf16[2,64,32768]{2,0,1:T(2,128)(2,1)} %slice.60) | data formatting | bytes 16777216 | tf_op jit(solution)/shard_map/reshape | solution.py:149
  618.9 7.8 copy.137
  631.9 85.3 %while.22 = (s32[]{:T(128)}, bf16[2,4,128,4,64]{2,1,0,4,3:T(4,128)(2,1)}, s32[2,4,9]{2,1,0:T(4,128)S(1)}, bf16[2,72,128,256]{3,2,1,0:T(8,128)(2,1)}, bf16[2,4,128,4,64]{2,4,3,1,0:T(8,128)(2,1)S(1)}, /*index=5*/s32[]{:T(128)}) while((s32[]{:T(128)}, bf16[2,4,128,4,64]{2,1,0,4,3:T(4,128)(2,1)}, s32[2,4,9]{2,1,0:T(4,128)S(1)}, ...), condition=%wide.region_5.8_spmd, body=%wide.region_2.7_spmd.sunk | while | flops 618269120 | bytes 66606568 | solution.py:94
  632.0 8.2 gather_fusion
  644.9 8.0 reshape.254
  657.0 9.3 %fusion.176 = (f32[4,4,128]{2,1,0:T(4,128)S(1)}, f32[4,4,128,1152]{3,2,1,0:T(8,128)}) fusion(bf16[4,1152,4,64]{3,2,1,0:T(4,128)(2,1)} %reshape.254, bf16[2,4,128,4,64]{2,4,3,1,0:T(8,128)(2,1)S(1)} %get-tuple-element.296, s32[]{:T(128)S(6)} %copy.206), kind=kOutput, calls=%fused_computation.129.clone.1 | convolution fusion | flops 309068928 | bytes 12066820 | tf_op jit(solution)/shard_map/while/body/eval_jaxpr/sub | solution.py:32
  674.7 8.2 gather_fusion
  687.6 8.0 reshape.254
  699.6 9.3 %fusion.176 = (f32[4,4,128]{2,1,0:T(4,128)S(1)}, f32[4,4,128,1152]{3,2,1,0:T(8,128)}) fusion(bf16[4,1152,4,64]{3,2,1,0:T(4,128)(2,1)} %reshape.254, bf16[2,4,128,4,64]{2,4,3,1,0:T(8,128)(2,1)S(1)} %get-tuple-element.296, s32[]{:T(128)S(6)} %copy.206), kind=kOutput, calls=%fused_computation.129.clone.1 | convolution fusion | flops 309068928 | bytes 12066820 | tf_op jit(solution)/shard_map/while/body/eval_jaxpr/sub | solution.py:32
  720.8 18.2 %copy.135 = f32[2,72,32768]{2,1,0:T(8,128)} copy(f32[2,72,32768]{2,0,1:T(2,128)} %get-tuple-element.73) | data formatting | bytes 37748736 | tf_op jit(solution)/shard_map/while | solution.py:142
  742.2 7.8 copy.138
  750.0 13.5 %reshape.172 = bf16[2,64,32768]{2,1,0:T(8,128)(2,1)} reshape(bf16[2,32,2,128,256]{4,3,2,1,0:T(8,128)(2,1)} %copy.138) | data formatting | bytes 16777216 | tf_op jit(solution)/shard_map/reshape | solution.py:158
  794.3 71.0 %reduce-scatter.8.cloned.1.call-done = bf16[32,1024]{1,0:T(8,128)(2,1)} async-done(((bf16[1024,1024]{1,0:T(8,128)(2,1)}), bf16[32,1024]{1,0:T(8,128)(2,1)}) %reduce-scatter.8.cloned.1.call-update) | async-done | bytes 65552 | tf_op jit(solution)/shard_map/reduce_scatter | solution.py:171
  868.2 28.4 %reduce-scatter.6.cloned.1.call-done = bf16[1024,256]{1,0:T(8,128)(2,1)} async-done(((bf16[1024,1024]{1,0:T(8,128)(2,1)}), bf16[1024,256]{1,0:T(8,128)(2,1)}) %reduce-scatter.6.cloned.1.call-update) | async-done | bytes 524304 | tf_op jit(solution)/shard_map/reduce_scatter | solution.py:189
  898.4 8.7 all-reduce
  (150 shorter events, 178.3 us)
Async XLA Ops:
  7.2 90.0 %copy-start = (bf16[256,1024]{1,0:T(8,128)(2,1)S(1)}, bf16[256,1024]{1,0:T(8,128)(2,1)}, u32[]{:S(2)}) copy-start(bf16[256,1024]{1,0:T(8,128)(2,1)} %param.16) | copy-start | bytes 1572868
  7.2 16.6 %copy-start.2 = (bf16[1024,1024]{1,0:T(8,128)(2,1)S(1)}, bf16[1024,1024]{1,0:T(8,128)(2,1)}, u32[]{:S(2)}) copy-start(bf16[1024,1024]{1,0:T(8,128)(2,1)} %param.14) | copy-start | bytes 6291460
  8.7 20.2 %all-to-all-start = ((s32[32,1,2]{2,1,0:T(1,128)}), s32[32,1,2]{2,1,0:T(1,128)S(1)}, u32[]{:S(2)}, u32[]{:S(2)}) async-start(s32[32,1,2]{2,1,0:T(1,128)} %copy.125), calls=%async_computation | async-start | bytes 32768 | tf_op jit(solution)/shard_map/all_to_all | solution.py:72
  18.9 8.3 copy-start.13
  21.2 6.0 copy-start.11
  27.2 1.2 copy-start.4
  30.2 5.4 copy-start.15
  50.9 8.4 slice-start
  51.0 113.5 %all-to-all-start.1 = ((bf16[2,32,2,128,256]{4,3,2,0,1:T(8,128)(2,1)}), bf16[2,32,2,128,256]{4,3,2,0,1:T(8,128)(2,1)}, u32[]{:S(2)}, u32[]{:S(2)}) async-start(bf16[2,32,2,128,256]{4,3,2,0,1:T(8,128)(2,1)} %copy.127), calls=%async_computation.1 | async-start | bytes 16777216 | tf_op jit(solution)/shard_map/all_to_all | solution.py:77
  58.6 38.6 %all-gather.2.cloned.1.call-start = ((), (), s32[]{:S(2)}) async-start(), calls=%async_computation.7 | async-start | bytes 2621440 | tf_op jit(solution)/shard_map/all_gather | solution.py:101
  180.1 6.7 copy-start.10
  219.7 7.8 copy-start.1
  423.8 7.8 copy-start.1
  626.7 5.2 copy-start.7
  626.7 115.5 %all-to-all-start.2 = ((bf16[2,32,2,128,256]{4,3,2,0,1:T(8,128)(2,1)}), bf16[2,32,2,128,256]{4,3,2,0,1:T(8,128)(2,1)}, u32[]{:S(2)}, u32[]{:S(2)}) async-start(bf16[2,32,2,128,256]{4,3,2,0,1:T(8,128)(2,1)} %copy.137), calls=%async_computation.3 | async-start | bytes 16777216 | tf_op jit(solution)/shard_map/all_to_all | solution.py:151
  631.8 160.5 %reduce-scatter.4.cloned.1.call-start = ((), (), s32[]{:S(2)}) async-start(), calls=%async_computation.6 | async-start | bytes 2621440 | tf_op jit(solution)/shard_map/reduce_scatter | solution.py:96
  666.3 7.2 copy-start.8
  673.8 0.8 copy-start.9
  708.9 7.2 copy-start.8
  716.4 0.8 copy-start.9
  720.7 144.6 %reduce-scatter.8.cloned.1.call-start = ((), (), s32[]{:S(2)}) async-start(), calls=%async_computation.9 | async-start | bytes 2162688 | tf_op jit(solution)/shard_map/reduce_scatter | solution.py:171
  720.8 18.2 %copy-start.17 = (bf16[1024,1024]{1,0:T(8,128)(2,1)S(1)}, bf16[1024,1024]{1,0:T(8,128)(2,1)}, u32[]{:S(2)}) copy-start(bf16[1024,1024]{1,0:T(8,128)(2,1)} %all-gather.2.cloned.1.call-done) | copy-start | bytes 6291460
  738.9 1.0 copy-start.6
  750.0 13.5 %copy-start.16 = (s32[64]{0:T(128)S(1)}, s32[64]{0:T(128)}, u32[]{:S(2)}) copy-start(s32[64]{0:T(128)} %copy-done.15) | copy-start | bytes 772
  763.5 10.9 %copy-start.3 = (bf16[1024,1024]{1,0:T(8,128)(2,1)S(1)}, bf16[1024,1024]{1,0:T(8,128)(2,1)}, u32[]{:S(2)}) copy-start(bf16[1024,1024]{1,0:T(8,128)(2,1)} %param.14) | copy-start | bytes 6291460
  763.5 10.9 %copy-start.12 = (f32[1024]{0:T(1024)S(1)}, f32[1024]{0:T(1024)}, u32[]{:S(2)}) copy-start(f32[1024]{0:T(1024)} %copy-done.11) | copy-start | bytes 12292
  763.5 10.9 %copy-start.14 = (f32[1024]{0:T(1024)S(1)}, f32[1024]{0:T(1024)}, u32[]{:S(2)}) copy-start(f32[1024]{0:T(1024)} %copy-done.13) | copy-start | bytes 12292
  784.7 112.0 %reduce-scatter.6.cloned.1.call-start = ((), (), s32[]{:S(2)}) async-start(), calls=%async_computation.8 | async-start | bytes 2621440 | tf_op jit(solution)/shard_map/reduce_scatter | solution.py:189
  789.9 117.3 %copy-start.5 = (bf16[1024,256]{1,0:T(8,128)(2,1)S(1)}, bf16[1024,256]{1,0:T(8,128)(2,1)}, u32[]{:S(2)}) copy-start(bf16[1024,256]{1,0:T(8,128)(2,1)} %param.19) | copy-start | bytes 1572868
Sparse Core Ops, SparseCore 0:
  61.1 36.0 all-gather.1
  720.8 31.2 reduce-scatter.3
  784.8 80.4 reduce-scatter.7
  867.7 28.9 reduce-scatter.5
where the time goes:
time: 930 us; the launch traced here: 917 us
  local copies, waits for them, and re-layouts  322 us (35%)
  waiting for transfers between devices  201 us (22%)
  matrix products  198 us (21%)
  other arithmetic  152 us (16%)
  starting transfers between devices  21.2 us (2%)
  between operations  14.3 us (2%)
    scatter-add x2, other arithmetic, backward_block(): return (totals.at[:, flat_entries].add(both_grads), grad_query)  97.6 us
    reduce_scatter x1, waiting for transfers between devices, on_device(): lax.psum_scatter(jnp.concatenate([input_part.reshape(model_width // peer_...  71 us
    all_to_all x1, waiting for transfers between devices, on_device(): lax.all_to_all(outgoing, 'space', split_axis=1, concat_axis=1, tiled=True)  64 us
    dot_general x2, matrix products, backward_block(): jnp.einsum('bhij,bihe->bjhe', grad_score, block_queries, preferred_elemen...  50.2 us
    dot_general x2, matrix products, backward_block(): jnp.einsum('bhij,bjhe->bihe', grad_score, key_part, preferred_element_typ...  47.5 us
    reshape x4, local copies, waits for them, and re-layouts, backward_block(): jnp.stack([grad_key.reshape(entry_count, -1), grad_value.reshape(entry_co...  41.3 us
    all_gather x1, waiting for transfers between devices, on_device(): cotangent_full = lax.all_gather(cotangent, 'head', axis=1, tiled=True)  36.5 us
    sub x4, matrix products, probabilities(): weights = jnp.exp(scores - row_top)  33.2 us
  transfers between devices with their start and end apart: 7, of which 4 were waited for; matrix products, arithmetic and copies ran while one was open for 19% of the time, Pallas kernels for 0%

commit v1 on v0

--- a/solution.py
+++ b/solution.py
@@ -98,7 +98,9 @@
     ).astype(jnp.float32)
     own_tokens = lax.dynamic_slice_in_dim(tokens, column, col_share, 1).astype(jnp.float32)
     layer_out = (own_tokens + summed).astype(jnp.bfloat16)
-    cotangent_full = lax.all_gather(cotangent, "head", axis=1, tiled=True)
+    cotangent_full = jnp.concatenate(
+        lax.all_to_all(jnp.stack([cotangent] * lax.axis_size("head")), "head", 0, 0), axis=1
+    )
     grad_attended = jnp.einsum(
         "td,fd->tf", cotangent_full, w_out, preferred_element_type=jnp.float32
     ).astype(jnp.bfloat16)

time: 930 us -> 943 us (1.014)
    all_to_all x1, waiting for transfers between devices: 64 us -> 101 us  [on_device(): lax.all_to_all(outgoing, 'space', split_axis=1, concat_axis=1, tiled=True)]
    all_gather x1 -> x0, waiting for transfers between devices: 36.5 us -> none  [on_device(): cotangent_full = lax.all_gather(cotangent, 'head', axis=1, tiled=True)]
  transfers between devices with their start and end apart: 7 -> 7, of which waited for: 4 -> 4; matrix products, arithmetic and copies ran while one was open for 19% -> 22% of each run, Pallas kernels for 0% -> 0%
where the time goes in v1:
time: 943 us; the launch traced here: 930 us
  local copies, waits for them, and re-layouts  324 us (34%)
  waiting for transfers between devices  204 us (22%)
  matrix products  201 us (21%)
  other arithmetic  152 us (16%)
  starting transfers between devices  25.3 us (3%)
  between operations  14.2 us (2%)
    all_to_all x1, waiting for transfers between devices, on_device(): lax.all_to_all(outgoing, 'space', split_axis=1, concat_axis=1, tiled=True)  101 us
    scatter-add x2, other arithmetic, backward_block(): return (totals.at[:, flat_entries].add(both_grads), grad_query)  97.6 us
    reduce_scatter x1, waiting for transfers between devices, on_device(): lax.psum_scatter(jnp.concatenate([input_part.reshape(model_width // peer_...  69.1 us
    dot_general x2, matrix products, backward_block(): jnp.einsum('bhij,bihe->bjhe', grad_score, block_queries, preferred_elemen...  50.2 us
    dot_general x2, matrix products, backward_block(): jnp.einsum('bhij,bjhe->bihe', grad_score, key_part, preferred_element_typ...  47.5 us
    reshape x4, local copies, waits for them, and re-layouts, backward_block(): jnp.stack([grad_key.reshape(entry_count, -1), grad_value.reshape(entry_co...  41.3 us
    sub x4, matrix products, probabilities(): weights = jnp.exp(scores - row_top)  33.2 us
    gather x4, local copies, waits for them, and re-layouts, gather_keys(): picked = jnp.take(extended, block_entries.reshape(-1), axis=1)  32.9 us
  transfers between devices with their start and end apart: 7, of which 4 were waited for; matrix products, arithmetic and copies ran while one was open for 22% of the time, Pallas kernels for 0%

profile of v1, /device:TPU:0, one launch (start us, length us, event | category | flops | bytes accessed | tf_op | source)
XLA Modules:
  0.0 929.5 jit_solution(7278678865462353794)
XLA Ops:
  8.7 8.2 all-to-all-start
  44.2 7.6 bitcast_select_fusion
  51.8 7.7 copy.130
  64.7 7.4 all-to-all-start.1
  76.7 101.2 %all-to-all-done.1 = bf16[2,32,2,128,256]{4,3,2,0,1:T(8,128)(2,1)} async-done(((bf16[2,32,2,128,256]{4,3,2,0,1:T(8,128)(2,1)}), bf16[2,32,2,128,256]{4,3,2,0,1:T(8,128)(2,1)}, u32[]{:S(2)}, u32[]{:S(2)}) %all-to-all-start.1) | async-done | bytes 8388640 | tf_op jit(solution)/shard_map/all_to_all | solution.py:77
  177.9 7.7 copy.131
  185.6 7.8 pad_maximum_fusion
  200.2 408.7 %while.23 = (s32[]{:T(128)}, f32[2,72,32768]{2,0,1:T(2,128)}, bf16[2,4,128,4,64]{2,4,3,1,0:T(8,128)(2,1)}, s32[2,4,9]{2,1,0:T(4,128)S(1)}, bf16[2,4,128,4,64]{2,...) while((s32[]{:T(128)}, f32[2,72,32768]{2,0,1:T(2,128)}, ...), condition=%wide.region_12.15_spmd, body=%wide.region_7.14_spmd.sunk | while | flops 1868574720 | bytes 270851232 | solution.py:144
  200.6 8.2 gather_fusion.1
  213.5 8.0 reshape.272
  221.5 7.5 copy.201
  233.1 7.8 fusion.195
  248.1 23.7 %fusion.197 = bf16[2,4,128,4,64]{2,4,3,1,0:T(8,128)(2,1)} fusion(bf16[2,4,128,4,64]{2,4,3,1,0:T(8,128)(2,1)} %get-tuple-element.308, s32[]{:T(128)S(6)} %copy.217, bf16[4,1152,4,64]{1,3,2,0:T(8,128)(2,1)S(1)} %copy-done.1, f32[4,4,128,1152]{3,2,1,0:T(8,128)} %fusion.195, f32[4,4,128,1152]{3,2,1,0:T(8,128)} %get-tuple-element.279, ...), kind=kOutput, calls=%fused_computation.52.clone.1 | convolution fusion | flops 318508160 | bytes 40648708 | tf_op jit(solution)/shard_map/while/body/eval_jaxpr/bhij,bjhe->bihe/dot_general | solution.py:127
  271.9 25.1 %fusion.196 = f32[4,1152,4,64]{1,3,2,0:T(8,128)} fusion(f32[4,4,128,1152]{3,2,1,0:T(8,128)} %fusion.195, bf16[2,4,128,4,64]{2,4,3,1,0:T(8,128)(2,1)} %get-tuple-element.318, s32[]{:T(128)S(6)} %copy.217, f32[4,4,128,1152]{3,2,1,0:T(8,128)} %get-tuple-element.279, f32[4,4,128]{2,1,0:T(4,128)S(1)} %get-tuple-element.277), kind=kOutput, calls=%fused_computation.50.clone.1 | convolution fusion | flops 318508160 | bytes 42745860 | tf_op jit(solution)/shard_map/while/body/eval_jaxpr/bhij,bihe->bjhe/dot_general | solution.py:130
  303.2 9.5 %copy.202 = f32[4,1152,4,64]{3,2,1,0:T(4,128)} copy(f32[4,1152,4,64]{1,3,2,0:T(8,128)} %fusion.194) | data formatting | bytes 9437184 | tf_op jit(solution)/shard_map/while/body/eval_jaxpr/bhij,bihe->bjhe/transpose | solution.py:133
  312.8 10.3 %reshape.273 = f32[1,36,32768]{2,1,0:T(8,128)} reshape(f32[4,1152,4,64]{3,2,1,0:T(4,128)} %copy.202) | data formatting | bytes 9437184 | tf_op jit(solution)/shard_map/while/body/eval_jaxpr/stack;while/body/eval_jaxpr/reshape | solution.py:138
  323.1 9.5 %copy.203 = f32[4,1152,4,64]{3,2,1,0:T(4,128)} copy(f32[4,1152,4,64]{1,3,2,0:T(8,128)} %fusion.196) | data formatting | bytes 9437184 | tf_op jit(solution)/shard_map/while/body/eval_jaxpr/bhij,bihe->bjhe/transpose | solution.py:130
  332.6 10.3 %reshape.275 = f32[1,36,32768]{2,1,0:T(8,128)} reshape(f32[4,1152,4,64]{3,2,1,0:T(4,128)} %copy.203) | data formatting | bytes 9437184 | tf_op jit(solution)/shard_map/while/body/eval_jaxpr/stack;while/body/eval_jaxpr/reshape | solution.py:138
  347.7 7.9 copy.204
  355.6 48.8 %scatter_fusion = f32[2,72,32768]{2,0,1:T(2,128)} fusion(f32[2,72,32768]{2,0,1:T(2,128)} %get-tuple-element.307, s32[36]{0:T(128)S(1)} %fusion.191, f32[36,2,32768]{2,1,0:T(2,128)} %copy.204), kind=kCustom, calls=%fused_computation.3.clone.1 | custom fusion | flops 2359296 | bytes 28311696 | tf_op jit(solution)/shard_map/while/body/eval_jaxpr/scatter-add | solution.py:141
  404.6 8.2 gather_fusion.1
  417.5 8.0 reshape.272
  425.5 7.5 copy.201
  437.1 7.8 fusion.195
  452.2 23.7 %fusion.197 = bf16[2,4,128,4,64]{2,4,3,1,0:T(8,128)(2,1)} fusion(bf16[2,4,128,4,64]{2,4,3,1,0:T(8,128)(2,1)} %get-tuple-element.308, s32[]{:T(128)S(6)} %copy.217, bf16[4,1152,4,64]{1,3,2,0:T(8,128)(2,1)S(1)} %copy-done.1, f32[4,4,128,1152]{3,2,1,0:T(8,128)} %fusion.195, f32[4,4,128,1152]{3,2,1,0:T(8,128)} %get-tuple-element.279, ...), kind=kOutput, calls=%fused_computation.52.clone.1 | convolution fusion | flops 318508160 | bytes 40648708 | tf_op jit(solution)/shard_map/while/body/eval_jaxpr/bhij,bjhe->bihe/dot_general | solution.py:127
  475.9 25.1 %fusion.196 = f32[4,1152,4,64]{1,3,2,0:T(8,128)} fusion(f32[4,4,128,1152]{3,2,1,0:T(8,128)} %fusion.195, bf16[2,4,128,4,64]{2,4,3,1,0:T(8,128)(2,1)} %get-tuple-element.318, s32[]{:T(128)S(6)} %copy.217, f32[4,4,128,1152]{3,2,1,0:T(8,128)} %get-tuple-element.279, f32[4,4,128]{2,1,0:T(4,128)S(1)} %get-tuple-element.277), kind=kOutput, calls=%fused_computation.50.clone.1 | convolution fusion | flops 318508160 | bytes 42745860 | tf_op jit(solution)/shard_map/while/body/eval_jaxpr/bhij,bihe->bjhe/dot_general | solution.py:130
  507.3 9.5 %copy.202 = f32[4,1152,4,64]{3,2,1,0:T(4,128)} copy(f32[4,1152,4,64]{1,3,2,0:T(8,128)} %fusion.194) | data formatting | bytes 9437184 | tf_op jit(solution)/shard_map/while/body/eval_jaxpr/bhij,bihe->bjhe/transpose | solution.py:133
  516.8 10.3 %reshape.273 = f32[1,36,32768]{2,1,0:T(8,128)} reshape(f32[4,1152,4,64]{3,2,1,0:T(4,128)} %copy.202) | data formatting | bytes 9437184 | tf_op jit(solution)/shard_map/while/body/eval_jaxpr/stack;while/body/eval_jaxpr/reshape | solution.py:138
  527.1 9.5 %copy.203 = f32[4,1152,4,64]{3,2,1,0:T(4,128)} copy(f32[4,1152,4,64]{1,3,2,0:T(8,128)} %fusion.196) | data formatting | bytes 9437184 | tf_op jit(solution)/shard_map/while/body/eval_jaxpr/bhij,bihe->bjhe/transpose | solution.py:130
  536.6 10.3 %reshape.275 = f32[1,36,32768]{2,1,0:T(8,128)} reshape(f32[4,1152,4,64]{3,2,1,0:T(4,128)} %copy.203) | data formatting | bytes 9437184 | tf_op jit(solution)/shard_map/while/body/eval_jaxpr/stack;while/body/eval_jaxpr/reshape | solution.py:138
  551.8 7.9 copy.204
  559.7 48.8 %scatter_fusion = f32[2,72,32768]{2,0,1:T(2,128)} fusion(f32[2,72,32768]{2,0,1:T(2,128)} %get-tuple-element.307, s32[36]{0:T(128)S(1)} %fusion.191, f32[36,2,32768]{2,1,0:T(2,128)} %copy.204), kind=kCustom, calls=%fused_computation.3.clone.1 | custom fusion | flops 2359296 | bytes 28311696 | tf_op jit(solution)/shard_map/while/body/eval_jaxpr/scatter-add | solution.py:141
  608.9 9.4 %slice.60 = bf16[2,64,32768]{2,0,1:T(2,128)(2,1)} slice(f32[2,72,32768]{2,0,1:T(2,128)} %get-tuple-element.73), slice={[0:2], [8:72], [0:32768]} | slice | bytes 16777216 | tf_op jit(solution)/shard_map/slice | solution.py:149
  618.2 14.0 %reshape.235 = bf16[2,32,2,128,256]{4,3,0,2,1:T(8,128)(2,1)} reshape(bf16[2,64,32768]{2,0,1:T(2,128)(2,1)} %slice.60) | data formatting | bytes 16777216 | tf_op jit(solution)/shard_map/reshape | solution.py:151
  632.3 7.8 copy.141
  645.2 85.3 %while.22 = (s32[]{:T(128)}, bf16[2,4,128,4,64]{2,1,0,4,3:T(4,128)(2,1)}, s32[2,4,9]{2,1,0:T(4,128)S(1)}, bf16[2,72,128,256]{3,2,1,0:T(8,128)(2,1)}, bf16[2,4,128,4,64]{2,4,3,1,0:T(8,128)(2,1)S(1)}, /*index=5*/s32[]{:T(128)}) while((s32[]{:T(128)}, bf16[2,4,128,4,64]{2,1,0,4,3:T(4,128)(2,1)}, s32[2,4,9]{2,1,0:T(4,128)S(1)}, ...), condition=%wide.region_5.8_spmd, body=%wide.region_2.7_spmd.sunk | while | flops 618269120 | bytes 66606568 | solution.py:94
  645.4 8.2 gather_fusion
  658.3 8.0 reshape.264
  670.3 9.3 fusion.176
  688.0 8.2 gather_fusion
  700.9 8.0 reshape.264
  713.0 9.3 fusion.176
  734.1 18.1 %copy.139 = f32[2,72,32768]{2,1,0:T(8,128)} copy(f32[2,72,32768]{2,0,1:T(2,128)} %get-tuple-element.73) | data formatting | bytes 37748736 | tf_op jit(solution)/shard_map/while | solution.py:144
  757.0 7.8 copy.142
  764.8 13.5 %reshape.182 = bf16[2,64,32768]{2,1,0:T(8,128)(2,1)} reshape(bf16[2,32,2,128,256]{4,3,2,1,0:T(8,128)(2,1)} %copy.142) | data formatting | bytes 16777216 | tf_op jit(solution)/shard_map/reshape | solution.py:160
  809.1 69.1 %reduce-scatter.8.cloned.1.call-done = bf16[32,1024]{1,0:T(8,128)(2,1)} async-done(((bf16[1024,1024]{1,0:T(8,128)(2,1)}), bf16[32,1024]{1,0:T(8,128)(2,1)}) %reduce-scatter.8.cloned.1.call-update) | async-done | bytes 65552 | tf_op jit(solution)/shard_map/reduce_scatter | solution.py:173
  881.1 28.6 %reduce-scatter.6.cloned.1.call-done = bf16[1024,256]{1,0:T(8,128)(2,1)} async-done(((bf16[1024,1024]{1,0:T(8,128)(2,1)}), bf16[1024,256]{1,0:T(8,128)(2,1)}) %reduce-scatter.6.cloned.1.call-update) | async-done | bytes 524304 | tf_op jit(solution)/shard_map/reduce_scatter | solution.py:191
  911.4 8.7 all-reduce
  (147 shorter events, 185.4 us)
Async XLA Ops:
  7.2 66.2 %copy-start = (bf16[256,1024]{1,0:T(8,128)(2,1)S(1)}, bf16[256,1024]{1,0:T(8,128)(2,1)}, u32[]{:S(2)}) copy-start(bf16[256,1024]{1,0:T(8,128)(2,1)} %param.16) | copy-start | bytes 1572868
  7.2 16.7 %copy-start.2 = (bf16[1024,1024]{1,0:T(8,128)(2,1)S(1)}, bf16[1024,1024]{1,0:T(8,128)(2,1)}, u32[]{:S(2)}) copy-start(bf16[1024,1024]{1,0:T(8,128)(2,1)} %param.14) | copy-start | bytes 6291460
  8.7 22.8 %all-to-all-start = ((s32[32,1,2]{2,1,0:T(1,128)}), s32[32,1,2]{2,1,0:T(1,128)S(1)}, u32[]{:S(2)}, u32[]{:S(2)}) async-start(s32[32,1,2]{2,1,0:T(1,128)} %copy.128), calls=%async_computation | async-start | bytes 32768 | tf_op jit(solution)/shard_map/all_to_all | solution.py:72
  18.9 4.9 copy-start.12
  21.2 2.6 copy-start.10
  33.1 31.6 %all-to-all-start.2 = ((bf16[4,1024,256]{1,2,0:T(8,128)(2,1)}), bf16[4,1024,256]{1,2,0:T(8,128)(2,1)}, u32[]{:S(2)}, u32[]{:S(2)}) async-start(bf16[4,1024,256]{1,2,0:T(8,128)(2,1)} %stack.4), calls=%async_computation.3 | async-start | bytes 4194304 | tf_op jit(solution)/shard_map/all_to_all | solution.py:102
  38.9 5.4 copy-start.14
  59.6 12.5 %slice-start = ((bf16[1024,768]{0,1:T(8,128)(2,1)}), bf16[1024,256]{0,1:T(8,128)(2,1)S(1)}, s32[]{:S(2)}) async-start(bf16[1024,768]{0,1:T(8,128)(2,1)} %convolution_convert_fusion.1), calls=%async_computation.10 | async-start | bytes 1048576 | tf_op jit(solution)/shard_map/slice | solution.py:64
  64.7 113.3 %all-to-all-start.1 = ((bf16[2,32,2,128,256]{4,3,2,0,1:T(8,128)(2,1)}), bf16[2,32,2,128,256]{4,3,2,0,1:T(8,128)(2,1)}, u32[]{:S(2)}, u32[]{:S(2)}) async-start(bf16[2,32,2,128,256]{4,3,2,0,1:T(8,128)(2,1)} %copy.130), calls=%async_computation.1 | async-start | bytes 16777216 | tf_op jit(solution)/shard_map/all_to_all | solution.py:77
  193.4 6.7 copy-start.9
  233.1 7.8 copy-start.1
  437.1 7.8 copy-start.1
  640.0 5.2 copy-start.6
  640.0 117.0 %all-to-all-start.3 = ((bf16[2,32,2,128,256]{4,3,2,0,1:T(8,128)(2,1)}), bf16[2,32,2,128,256]{4,3,2,0,1:T(8,128)(2,1)}, u32[]{:S(2)}, u32[]{:S(2)}) async-start(bf16[2,32,2,128,256]{4,3,2,0,1:T(8,128)(2,1)} %copy.141), calls=%async_computation.4 | async-start | bytes 16777216 | tf_op jit(solution)/shard_map/all_to_all | solution.py:153
  645.2 161.9 %reduce-scatter.4.cloned.1.call-start = ((), (), s32[]{:S(2)}) async-start(), calls=%async_computation.7 | async-start | bytes 2621440 | tf_op jit(solution)/shard_map/reduce_scatter | solution.py:96
  679.6 7.2 copy-start.7
  687.1 0.8 copy-start.8
  722.2 7.2 copy-start.7
  729.8 0.8 copy-start.8
  734.0 144.1 %reduce-scatter.8.cloned.1.call-start = ((), (), s32[]{:S(2)}) async-start(), calls=%async_computation.9 | async-start | bytes 2162688 | tf_op jit(solution)/shard_map/reduce_scatter | solution.py:173
  752.2 2.6 copy-start.5
  764.8 13.5 %copy-start.15 = (s32[64]{0:T(128)S(1)}, s32[64]{0:T(128)}, u32[]{:S(2)}) copy-start(s32[64]{0:T(128)} %copy-done.14) | copy-start | bytes 772
  778.3 10.9 %copy-start.3 = (bf16[1024,1024]{1,0:T(8,128)(2,1)S(1)}, bf16[1024,1024]{1,0:T(8,128)(2,1)}, u32[]{:S(2)}) copy-start(bf16[1024,1024]{1,0:T(8,128)(2,1)} %param.14) | copy-start | bytes 6291460
  778.3 10.9 %copy-start.11 = (f32[1024]{0:T(1024)S(1)}, f32[1024]{0:T(1024)}, u32[]{:S(2)}) copy-start(f32[1024]{0:T(1024)} %copy-done.10) | copy-start | bytes 12292
  778.3 10.9 %copy-start.13 = (f32[1024]{0:T(1024)S(1)}, f32[1024]{0:T(1024)}, u32[]{:S(2)}) copy-start(f32[1024]{0:T(1024)} %copy-done.12) | copy-start | bytes 12292
  799.5 110.2 %reduce-scatter.6.cloned.1.call-start = ((), (), s32[]{:S(2)}) async-start(), calls=%async_computation.8 | async-start | bytes 2621440 | tf_op jit(solution)/shard_map/reduce_scatter | solution.py:191
  804.6 115.5 %copy-start.4 = (bf16[1024,256]{1,0:T(8,128)(2,1)S(1)}, bf16[1024,256]{1,0:T(8,128)(2,1)}, u32[]{:S(2)}) copy-start(bf16[1024,256]{1,0:T(8,128)(2,1)} %param.19) | copy-start | bytes 1572868
Sparse Core Ops, SparseCore 0:
  734.2 29.1 reduce-scatter.3
  799.6 78.4 reduce-scatter.7
  880.7 28.9 reduce-scatter.5
